TPU v7x, 128 devices: a whole 4x4x4 slice. The times are simulated.
128 devices in a mesh: site: 16 (over x, y_lo, core), mom: 8 (over y_hi, z).
Axes of the slice: x: 4, y: 4 (y_hi: 2, y_lo: 2; y = y_hi * 2 + y_lo), z: 4, core: 2. Of those that a mesh axis runs over, the one named last changes fastest.
Arguments:
- left_seeds: float32 [8, 2, 512, 1024], P('mom', None, 'site'), may hold values from -6 to 6
- right_seeds: float32 [8, 2, 512, 1024], P('mom', None, 'site'), may hold values from -6 to 6
- site_types: int32 [512, 1024], P('site'), may hold values from 0 to 3
- levels: float32 [4], replicated, may hold values from -1 to 1
Outputs:
- moments: float32 [256, 256], P('mom', 'site')
All inputs are finite; a program needn't handle non-finite values.
Results may differ from a plain program's by a relative error of at most 0.00011.
Values sent between devices are 32-bit elements; how exact they have to be, the bound alone decides.
A program may use at most 128 MiB of HBM per device.

v0:
```python
import math

import jax
import jax.numpy as jnp
from jax import lax
from jax.sharding import PartitionSpec as P

MB = 32


SCALE = 1.0 / 4.2


def extended(block, sides, width):
    for axis, dim in sides:
        count = lax.axis_size(axis)
        forward = [(i, i + 1) for i in range(count - 1)]
        backward = [(target, source) for source, target in forward]
        low = lax.ppermute(
            lax.slice_in_dim(block, block.shape[dim] - width, None, axis=dim), axis, forward
        )
        high = lax.ppermute(lax.slice_in_dim(block, 0, width, axis=dim), axis, backward)
        block = jnp.concatenate([low, block, high], axis=dim)
    return block


def from_behind(x, axis, by):
    devices = lax.axis_size(axis)
    return lax.ppermute(x, axis, [(i, (i + by) % devices) for i in range(devices)])


def on_device(left_seeds, right_seeds, site_types, levels):
    local_x = site_types.shape[0]
    width_y = site_types.shape[1]
    kinds = levels.shape[0]
    match = site_types[None, :, :] == jnp.arange(kinds, dtype=jnp.int32)[:, None, None]
    energy = jnp.sum(jnp.where(match, levels[:, None, None], jnp.float32(0.0)), axis=0)
    rows_x = lax.broadcasted_iota(jnp.int32, (local_x, width_y), 0)
    rows_y = lax.broadcasted_iota(jnp.int32, (local_x, width_y), 1)
    parity = (rows_x + rows_y) % 2 == 0

    def hamilton(current):
        padded = extended(current, (("site", 1),), 1)
        above = padded[:, 2:, :]
        below = padded[:, :-2, :]
        across = jnp.where(parity, jnp.roll(current, -1, axis=2), jnp.roll(current, 1, axis=2))
        return (energy * current + above + below + across) * SCALE

    first = jnp.stack([left_seeds[0, 0], right_seeds[0, 0]])
    second = jnp.stack([left_seeds[0, 1], right_seeds[0, 1]])

    def step(carry, unused):
        before, current = carry
        fresh = 2.0 * hamilton(current) - before
        return ((current, fresh), fresh)

    _, rest = lax.scan(step, (first, second), None, length=MB - 2)
    vectors = jnp.concatenate([first[None], second[None], rest], axis=0)
    left_cube = vectors[:, 0]
    left_block = left_cube.reshape(MB, local_x * width_y)
    cheb_block = vectors[:, 1]
    rimmed = extended(cheb_block, (("site", 1),), 1)
    right_cube = rimmed[:, 2:, :] - rimmed[:, :-2, :]
    right_block = right_cube.reshape(MB, local_x * width_y)
    blocks = lax.axis_size("mom")
    total_moments = MB * blocks
    own = lax.axis_index("mom")

    def product(right_piece):
        return jnp.dot(
            left_block,
            right_piece.T,
            precision=lax.Precision.HIGHEST,
            preferred_element_type=jnp.float32,
        )

    empty = jnp.zeros((MB, total_moments), jnp.float32)
    start_col = own * MB
    partial_sums = lax.dynamic_update_slice(empty, product(right_block), (jnp.int32(0), start_col))

    def turn(count, carry):
        sums_now, travel = carry
        travel = from_behind(travel, "mom", 1)
        source = (own - count) % blocks
        sums_now = lax.dynamic_update_slice(sums_now, product(travel), (jnp.int32(0), source * MB))
        return (sums_now, travel)

    partial_sums, _ = lax.fori_loop(1, blocks, turn, (partial_sums, right_block))
    total_x = local_x * lax.axis_size("site")
    owned = lax.psum_scatter(partial_sums, "site", scatter_dimension=1, tiled=True)
    return owned * (1.0 / math.sqrt(total_x * width_y))


def solution(mesh):
    return jax.shard_map(
        on_device,
        mesh=mesh,
        in_specs=(P("mom", None, "site", None), P("mom", None, "site", None), P("site", None), P()),
        out_specs=P("mom", "site"),
        check_vma=False,
    )
```

profile of v0, /device:TPU:1, one launch (start us, length us, event | category | flops | bytes accessed | tf_op | source)
XLA Modules:
  0.0 1120.5 jit_solution(15139755158202869733)
XLA Ops:
  9.7 264.9 %while.35 = (s32[]{:T(128)}, f32[2,32,1024]{2,1,0:T(8,128)S(1)}, f32[2,32,1024]{2,1,0:T(8,128)S(1)}, f32[30,2,32,1024]{3,2,1,0:T(8,128)}, f32[32,1024]{1,0:T(8,128)S(1)}, /*index=5*/s32[]{:T(128)}) while((s32[]{:T(128)}, f32[2,32,1024]{2,1,0:T(8,128)S(1)}, f32[2,32,1024]{2,1,0:T(8,128)S(1)}, f32[30,2,32,1024]{3,2,1,0:T(8,128)}, ...), condition=%wide.region_2.3_spmd.clone, body=%wide.region_1.2_spmd.clone.sunk | while | flops 1146882 | bytes 3981473 | solution.py:57
  9.7 4.6 collective-permute-start.1
  33.3 3.2 collective-permute-done.2
  42.1 3.2 collective-permute-done.2
  50.9 3.2 collective-permute-done.2
  59.7 3.2 collective-permute-done.2
  68.5 3.2 collective-permute-done.2
  77.2 3.2 collective-permute-done.2
  86.1 3.2 collective-permute-done.2
  94.8 3.2 collective-permute-done.2
  103.6 3.2 collective-permute-done.2
  112.4 3.2 collective-permute-done.2
  121.2 3.2 collective-permute-done.2
  130.0 3.2 collective-permute-done.2
  138.8 3.2 collective-permute-done.2
  147.5 3.2 collective-permute-done.2
  156.3 3.2 collective-permute-done.2
  165.1 3.2 collective-permute-done.2
  244.2 3.2 collective-permute-done.2
  274.6 3.7 pad_maximum_fusion.2
  278.3 3.2 slice_bitcast_fusion
  285.6 3.8 collective-permute-start.4
  289.5 6.6 copy.7
  296.1 4.7 fusion.12
  303.3 3.5 fusion.21
  307.3 743.9 %while.34 = (s32[]{:T(128)}, f32[32,256]{1,0:T(8,128)S(1)}, f32[32,32768]{1,0:T(8,128)}, f32[32,32768]{1,0:T(8,128)}, s32[]{:T(128)}, /*index=5*/s32[]{:T(128)},...) while((s32[]{:T(128)}, f32[32,256]{1,0:T(8,128)S(1)}, f32[32,32768]{1,0:T(8,128)}, ...), condition=%wide.region_4.5_spmd, body=%wide.region_3.4_spmd.sunk | while | flops 402653184 | bytes 33567032 | solution.py:88
  309.1 94.8 %collective-permute-done = f32[32,32768]{1,0:T(8,128)} collective-permute-done((f32[32,32768]{1,0:T(8,128)}, f32[32,32768]{1,0:T(8,128)}, u32[]{:S(2)}, u32[]{:S(2)}) %collective-permute-start) | collective-permute-done | bytes 4194336 | tf_op jit(solution)/shard_map/while/body/eval_jaxpr/ppermute | solution.py:29
  403.9 6.9 fusion.35
  411.2 4.4 copy.32
  415.7 96.4 %collective-permute-done = f32[32,32768]{1,0:T(8,128)} collective-permute-done((f32[32,32768]{1,0:T(8,128)}, f32[32,32768]{1,0:T(8,128)}, u32[]{:S(2)}, u32[]{:S(2)}) %collective-permute-start) | collective-permute-done | bytes 4194336 | tf_op jit(solution)/shard_map/while/body/eval_jaxpr/ppermute | solution.py:29
  512.1 6.9 fusion.35
  519.4 4.4 copy.32
  523.8 95.6 %collective-permute-done = f32[32,32768]{1,0:T(8,128)} collective-permute-done((f32[32,32768]{1,0:T(8,128)}, f32[32,32768]{1,0:T(8,128)}, u32[]{:S(2)}, u32[]{:S(2)}) %collective-permute-start) | collective-permute-done | bytes 4194336 | tf_op jit(solution)/shard_map/while/body/eval_jaxpr/ppermute | solution.py:29
  619.4 6.9 fusion.35
  626.7 4.4 copy.32
  631.1 94.6 %collective-permute-done = f32[32,32768]{1,0:T(8,128)} collective-permute-done((f32[32,32768]{1,0:T(8,128)}, f32[32,32768]{1,0:T(8,128)}, u32[]{:S(2)}, u32[]{:S(2)}) %collective-permute-start) | collective-permute-done | bytes 4194336 | tf_op jit(solution)/shard_map/while/body/eval_jaxpr/ppermute | solution.py:29
  725.7 6.9 fusion.35
  732.9 4.4 copy.32
  737.4 93.7 %collective-permute-done = f32[32,32768]{1,0:T(8,128)} collective-permute-done((f32[32,32768]{1,0:T(8,128)}, f32[32,32768]{1,0:T(8,128)}, u32[]{:S(2)}, u32[]{:S(2)}) %collective-permute-start) | collective-permute-done | bytes 4194336 | tf_op jit(solution)/shard_map/while/body/eval_jaxpr/ppermute | solution.py:29
  831.1 6.9 fusion.35
  838.5 4.4 copy.32
  842.9 92.8 %collective-permute-done = f32[32,32768]{1,0:T(8,128)} collective-permute-done((f32[32,32768]{1,0:T(8,128)}, f32[32,32768]{1,0:T(8,128)}, u32[]{:S(2)}, u32[]{:S(2)}) %collective-permute-start) | collective-permute-done | bytes 4194336 | tf_op jit(solution)/shard_map/while/body/eval_jaxpr/ppermute | solution.py:29
  935.7 6.9 fusion.35
  943.1 4.4 copy.32
  947.5 91.9 %collective-permute-done = f32[32,32768]{1,0:T(8,128)} collective-permute-done((f32[32,32768]{1,0:T(8,128)}, f32[32,32768]{1,0:T(8,128)}, u32[]{:S(2)}, u32[]{:S(2)}) %collective-permute-start) | collective-permute-done | bytes 4194336 | tf_op jit(solution)/shard_map/while/body/eval_jaxpr/ppermute | solution.py:29
  1039.4 6.9 fusion.35
  1046.8 4.4 copy.32
  1052.0 60.3 %reduce-scatter.2.cloned.1.call-done = f32[32,16]{0,1:T(8,128)} async-done(((f32[32,256]{0,1:T(8,128)}), f32[32,16]{0,1:T(8,128)}) %reduce-scatter.2.cloned.1.call-update) | async-done | bytes 2064 | tf_op jit(solution)/shard_map/reduce_scatter | solution.py:90
  (348 shorter events, 220.3 us)
Async XLA Ops:
  6.5 1105.8 %reduce-scatter.2.cloned.1.call-start = ((), (), s32[]{:S(2)}) async-start(), calls=%async_computation.1 | async-start | bytes 139264 | tf_op jit(solution)/shard_map/reduce_scatter | solution.py:90
  9.7 6.8 collective-permute-start.1
  14.3 5.0 collective-permute-start.2
  20.3 4.6 collective-permute-start.1
  22.2 5.6 collective-permute-start.2
  28.7 4.6 collective-permute-start.1
  30.7 5.9 collective-permute-start.2
  37.5 4.6 collective-permute-start.1
  39.5 5.9 collective-permute-start.2
  46.3 4.6 collective-permute-start.1
  48.2 5.9 collective-permute-start.2
  55.1 4.6 collective-permute-start.1
  57.0 5.9 collective-permute-start.2
  65.8 5.9 collective-permute-start.2
  74.6 5.9 collective-permute-start.2
  83.4 5.9 collective-permute-start.2
  92.2 5.9 collective-permute-start.2
  101.0 5.9 collective-permute-start.2
  109.8 5.9 collective-permute-start.2
  118.6 5.9 collective-permute-start.2
  125.4 4.6 collective-permute-start.1
  127.3 5.9 collective-permute-start.2
  136.1 5.9 collective-permute-start.2
  142.9 4.6 collective-permute-start.1
  144.9 5.9 collective-permute-start.2
  153.6 5.9 collective-permute-start.2
  162.4 5.9 collective-permute-start.2
  171.2 5.9 collective-permute-start.2
  180.0 5.9 collective-permute-start.2
  188.8 5.9 collective-permute-start.2
  197.5 5.9 collective-permute-start.2
  206.3 5.9 collective-permute-start.2
  215.1 5.9 collective-permute-start.2
  223.9 5.9 collective-permute-start.2
  232.7 5.9 collective-permute-start.2
  241.5 5.9 collective-permute-start.2
  250.3 5.9 collective-permute-start.2
  259.1 5.9 collective-permute-start.2
  267.8 5.9 collective-permute-start.2
  283.7 12.4 %collective-permute-start.3 = (f32[32,1,1024]{2,1,0:T(1,128)S(1)}, f32[32,1,1024]{2,1,0:T(1,128)S(1)}, u32[]{:S(2)}, u32[]{:S(2)}) collective-permute-start(f32[32,1,1024]{2,1,0:T(1,128)S(1)} %get-tuple-element.259), channel_id=1, source_target_pairs={{8,0},{16,8},{24,16},{32,24},{40,32},{48,40},{56,48},{64,56},{72,6... | collective-permute-start | bytes 393224 | tf_op jit(solution)/shard_map/ppermute | solution.py:22
  285.6 10.4 collective-permute-start.4
  307.3 96.6 %collective-permute-start = (f32[32,32768]{1,0:T(8,128)}, f32[32,32768]{1,0:T(8,128)}, u32[]{:S(2)}, u32[]{:S(2)}) collective-permute-start(f32[32,32768]{1,0:T(8,128)} %get-tuple-element.380), channel_id=1, source_target_pairs={{0,1},{1,2},{2,3},{3,4},{4,5},{5,6},{6,7},{7,0},{8,9},{9,10},{10,1... | collective-permute-start | bytes 12582920 | tf_op jit(solution)/shard_map/while/body/eval_jaxpr/ppermute | solution.py:29
  415.6 96.4 %collective-permute-start = (f32[32,32768]{1,0:T(8,128)}, f32[32,32768]{1,0:T(8,128)}, u32[]{:S(2)}, u32[]{:S(2)}) collective-permute-start(f32[32,32768]{1,0:T(8,128)} %get-tuple-element.380), channel_id=1, source_target_pairs={{0,1},{1,2},{2,3},{3,4},{4,5},{5,6},{6,7},{7,0},{8,9},{9,10},{10,1... | collective-permute-start | bytes 12582920 | tf_op jit(solution)/shard_map/while/body/eval_jaxpr/ppermute | solution.py:29
  523.8 95.6 %collective-permute-start = (f32[32,32768]{1,0:T(8,128)}, f32[32,32768]{1,0:T(8,128)}, u32[]{:S(2)}, u32[]{:S(2)}) collective-permute-start(f32[32,32768]{1,0:T(8,128)} %get-tuple-element.380), channel_id=1, source_target_pairs={{0,1},{1,2},{2,3},{3,4},{4,5},{5,6},{6,7},{7,0},{8,9},{9,10},{10,1... | collective-permute-start | bytes 12582920 | tf_op jit(solution)/shard_map/while/body/eval_jaxpr/ppermute | solution.py:29
  631.1 94.6 %collective-permute-start = (f32[32,32768]{1,0:T(8,128)}, f32[32,32768]{1,0:T(8,128)}, u32[]{:S(2)}, u32[]{:S(2)}) collective-permute-start(f32[32,32768]{1,0:T(8,128)} %get-tuple-element.380), channel_id=1, source_target_pairs={{0,1},{1,2},{2,3},{3,4},{4,5},{5,6},{6,7},{7,0},{8,9},{9,10},{10,1... | collective-permute-start | bytes 12582920 | tf_op jit(solution)/shard_map/while/body/eval_jaxpr/ppermute | solution.py:29
  737.4 93.7 %collective-permute-start = (f32[32,32768]{1,0:T(8,128)}, f32[32,32768]{1,0:T(8,128)}, u32[]{:S(2)}, u32[]{:S(2)}) collective-permute-start(f32[32,32768]{1,0:T(8,128)} %get-tuple-element.380), channel_id=1, source_target_pairs={{0,1},{1,2},{2,3},{3,4},{4,5},{5,6},{6,7},{7,0},{8,9},{9,10},{10,1... | collective-permute-start | bytes 12582920 | tf_op jit(solution)/shard_map/while/body/eval_jaxpr/ppermute | solution.py:29
  842.9 92.8 %collective-permute-start = (f32[32,32768]{1,0:T(8,128)}, f32[32,32768]{1,0:T(8,128)}, u32[]{:S(2)}, u32[]{:S(2)}) collective-permute-start(f32[32,32768]{1,0:T(8,128)} %get-tuple-element.380), channel_id=1, source_target_pairs={{0,1},{1,2},{2,3},{3,4},{4,5},{5,6},{6,7},{7,0},{8,9},{9,10},{10,1... | collective-permute-start | bytes 12582920 | tf_op jit(solution)/shard_map/while/body/eval_jaxpr/ppermute | solution.py:29
  947.5 91.9 %collective-permute-start = (f32[32,32768]{1,0:T(8,128)}, f32[32,32768]{1,0:T(8,128)}, u32[]{:S(2)}, u32[]{:S(2)}) collective-permute-start(f32[32,32768]{1,0:T(8,128)} %get-tuple-element.380), channel_id=1, source_target_pairs={{0,1},{1,2},{2,3},{3,4},{4,5},{5,6},{6,7},{7,0},{8,9},{9,10},{10,1... | collective-permute-start | bytes 12582920 | tf_op jit(solution)/shard_map/while/body/eval_jaxpr/ppermute | solution.py:29
  (25 other events, 109.1 us)
Sparse Core Ops, SparseCore 0:
  1052.1 60.1 reduce-scatter.1
where the time goes:
time: 1130 us; the launch traced here: 1120 us
  waiting for transfers between devices  816 us (72%)
  starting transfers between devices  139 us (12%)
  local copies, waits for them, and re-layouts  59.1 us (5%)
  matrix products  52 us (5%)
  other arithmetic  38.1 us (3%)
  between operations  13.5 us (1%)
    ppermute x7, waiting for transfers between devices, from_behind(): lax.ppermute(x, axis, [(i, (i + by) % devices) for i in range(devices)])  660 us
    ppermute x31, waiting for transfers between devices, extended(): lax.ppermute(lax.slice_in_dim(block, 0, width, axis=dim), axis, backward)  95.8 us
    ppermute x31, starting transfers between devices, extended(): lax.ppermute(lax.slice_in_dim(block, 0, width, axis=dim), axis, backward)  72.8 us
    ppermute x31, starting transfers between devices, extended(): lax.ppermute(lax.slice_in_dim(block, block.shape[dim] - width, None, axis...  64.8 us
    reduce_scatter x1, waiting for transfers between devices, on_device(): lax.psum_scatter(partial_sums, 'site', scatter_dimension=1, tiled=True)  60.3 us
    dot_general x8, matrix products, product(): jnp.dot(left_block, right_piece.T, precision=lax.Precision.HIGHEST, prefe...  52 us
    while x67, local copies, waits for them, and re-layouts  32.1 us
    dynamic_update_slice x30, other arithmetic, on_device(): _, rest = lax.scan(step, (first, second), None, length=MB - 2)  26.2 us
  transfers between devices with their start and end apart: 70, of which 38 were waited for; matrix products, arithmetic and copies ran while one was open for 1% of the time, Pallas kernels for 0%

commit v1 on v0

v1 whole, which is shorter than its diff:
```python
import functools
import math

import jax
import jax.numpy as jnp
from jax import lax
from jax.experimental import pallas as pl
from jax.experimental.pallas import tpu as pltpu
from jax.sharding import PartitionSpec as P

MB = 32
HOP = 2.0 / 4.2
MESH = pl.DeviceIdType.MESH
F32 = jnp.float32
BF16 = jnp.bfloat16
LANES = 128
HALF = 64
EDGE = 8
PAD = 4
PHASES = 5


def snake(b):
    return jnp.where(b < 4, b, 11 - b)


def lanes_of(rows):
    return lax.broadcasted_iota(jnp.int32, (rows, LANES), 1)


def pieces(x):
    high = x.astype(BF16)
    rest = x - high.astype(F32)
    middle = rest.astype(BF16)
    low = (rest - middle.astype(F32)).astype(BF16)
    return jnp.concatenate([high, middle, low], axis=1)


def unzip(x):
    row = lax.broadcasted_iota(jnp.int32, (3 * LANES, LANES), 0) % LANES
    col = lax.broadcasted_iota(jnp.int32, (3 * LANES, LANES), 1)
    source = jnp.where(col < HALF, 2 * col, 2 * (col - HALF) + 1)
    matrix = jnp.where(row == source, 1.0, 0.0).astype(BF16)
    return jnp.dot(pieces(x), matrix, preferred_element_type=F32)


def spread_energy(ebuf, energy):
    lane = lanes_of(32)
    for tile in range(3):
        own = ebuf[tile, 1]
        halo = jnp.where(lane % HALF < 32, pltpu.roll(ebuf[tile, 2], HALF, 1), pltpu.roll(ebuf[tile, 0], HALF, 1))
        for v in range(2):
            value = jnp.where(lane < HALF, own, halo) if v == 0 else jnp.where(lane < HALF, halo, own)
            for r in range(32):
                energy[PAD + 32 * tile + r, v] = jnp.broadcast_to(value[r:r + 1, :], (8, LANES))


def fill(lr, t, xbuf, ybuf, state):
    lane = lanes_of(8)
    inner = lane < HALF
    for tile in range(3):
        xs = xbuf.at[tile, lr].reshape(8 * 2 * 32, LANES)
        y0 = ybuf.at[tile, lr, 0].reshape(64, LANES)
        y1 = ybuf.at[tile, lr, 1].reshape(64, LANES)
        for r in range(8):
            low = y0[pl.ds(r, 8, stride=8), :]
            high = y1[pl.ds(r, 8, stride=8), :]
            for f in range(2):
                for g in range(4):
                    slot = f * 4 + g
                    row = 32 * tile + 8 * g + r
                    own = xs[pl.ds(f * 32 + 8 * g + r, 8, stride=64), :]
                    halo = jnp.where(
                        lane % HALF < 32,
                        pltpu.roll(high, HALF - EDGE * slot, 1),
                        pltpu.roll(low, LANES - EDGE - EDGE * slot, 1))
                    pair = (jnp.where(inner, own, halo), jnp.where(inner, halo, own))
                    for v in range(2):
                        new = pair[v]
                        if row == 31:
                            new = jnp.where(t == 0, 0.0, new)
                        if row == 64:
                            new = jnp.where(t == 15, 0.0, new)
                        state[f, PAD + row, v] = new


def step(lr, t, k, p, low, high, state, energy, arch):
    lane = lanes_of(8)
    load = lambda row: [state[p, PAD + row, v] for v in range(2)]
    below, here = load(low - 1), load(low)
    for row in range(low, high):
        above = load(row + 1)
        turn = (HALF, HALF) if row % 2 == 0 else (HALF + 1, HALF - 1)
        for v in range(2):
            across = pltpu.roll(here[1 - v], turn[v], 1)
            new = (energy[PAD + row, v] * here[v]
                   + (above[v] + below[v] + across) * HOP - state[1 - p, PAD + row, v])
            if row == 31:
                new = jnp.where(t == 0, 0.0, new)
            if row == 64:
                new = jnp.where(t == 15, 0.0, new)
            state[1 - p, PAD + row, v] = new
        if 32 <= row < 64:
            keep(lr, lane, row, k, below, here, above, arch)
        below, here = here, above


def keep(lr, lane, row, k, below, here, above, arch):
    join = lambda x: jnp.where(lane < HALF, x[0], x[1])
    mine = join(above) - join(below) if lr else join(here)
    arch[lr, row - 32, pl.ds(pl.multiple_of(8 * k, 8), 8), :] = mine


def save(lr, k, p, state, arch):
    lane = lanes_of(8)
    for row in range(32, 64):
        load = lambda i: [state[p, PAD + row + i, v] for v in range(2)]
        keep(lr, lane, row, k, load(-1), load(0), load(1), arch)


def run(lr, t, state, energy, arch):
    save(lr, 0, 0, state, arch)
    pairs = 15 // PHASES
    for phase in range(PHASES):
        first = 2 * pairs * phase

        def double(i, unused):
            k = first + 2 * i + 1
            step(lr, t, k, 1, first + 1, 95 - first, state, energy, arch)
            step(lr, t, k + 1, 0, first + 2, 94 - first, state, energy, arch)
            return unused

        lax.fori_loop(0, pairs, double, 0)
    save(lr, 31, 1, state, arch)


def gram(arch, sums):
    sums[...] = jnp.zeros_like(sums)

    def halves(lr, r):
        x = jnp.concatenate(
            [jnp.concatenate([arch[lr, r + i, pl.ds(q, 32, stride=8), :] for q in range(8)], axis=0)
             for i in range(2)], axis=1)
        high = x.astype(BF16)
        return high, (x - high.astype(F32)).astype(BF16)

    def product(a, c):
        return lax.dot_general(a, c, (((1,), (1,)), ((), ())), preferred_element_type=F32)

    def add(i, unused):
        lh, ll = halves(0, 2 * i)
        rh, rl = halves(1, 2 * i)
        sums[...] += product(rh, lh) + product(rh, ll) + product(rl, lh)
        return unused

    lax.fori_loop(0, 16, add, 0)


def kernel(scale, left_ref, right_ref, types_ref, levels, out,
           raw, types, seeds, xbuf, ybuf, ebuf, pack, state, energy, arch, sums, got, turned, parts,
           in_sem, a_send, a_recv, own_sem, x_send, x_recv, y_send, y_recv, e_send, e_recv,
           s_send, s_recv, m_send, m_recv):
    t = lax.axis_index("site")
    b = lax.axis_index("mom")
    c = snake(b)
    has_low = t > 0
    has_high = t < 15
    mom_right = snake(lax.rem(c + 1, 8))
    mom_left = snake(lax.rem(c + 7, 8))

    loads = [pltpu.make_async_copy(left_ref.at[0], raw.at[0], in_sem.at[0]),
             pltpu.make_async_copy(right_ref.at[0], raw.at[1], in_sem.at[1]),
             pltpu.make_async_copy(types_ref, types, in_sem.at[2])]
    for load in loads:
        load.start()

    barrier = pltpu.get_barrier_semaphore()
    for j in range(1, 8):
        pl.semaphore_signal(barrier, inc=1, device_id=(t, lax.rem(b + j, 8)), device_id_type=MESH)
    for j in range(1, 16):
        pl.semaphore_signal(barrier, inc=1, device_id=(lax.rem(t + j, 16), b), device_id_type=MESH)
    for there, dt in ((has_low, -1), (has_high, 1)):
        @pl.when(there)
        def _():
            for q in (mom_left, mom_right):
                pl.semaphore_signal(barrier, inc=1, device_id=(t + dt, q), device_id_type=MESH)

    def unzip_seeds(lr):
        x = jnp.concatenate(
            [raw[lr, :, :, LANES * i:LANES * i + LANES].reshape(64, LANES) for i in range(8)], axis=0)
        seeds[lr] = unzip(x).reshape(8, 2, 32, LANES)

    loads[0].wait()
    unzip_seeds(0)
    pl.semaphore_wait(barrier, 22 + jnp.where(has_low, 2, 0) + jnp.where(has_high, 2, 0))

    def a_copy(lr, j):
        q = lax.rem(b + j, 8)
        return pltpu.make_async_remote_copy(
            src_ref=seeds.at[lr, snake(q)], dst_ref=xbuf.at[1, lr, b],
            send_sem=a_send.at[lr, j], recv_sem=a_recv.at[lr, j],
            device_id=(t, q), device_id_type=MESH)

    def a_arrival(lr, j):
        q = lax.rem(b + 8 - j, 8)
        return q, pltpu.make_async_remote_copy(
            src_ref=xbuf.at[1, lr, q], dst_ref=xbuf.at[1, lr, q],
            send_sem=a_send.at[lr, j], recv_sem=a_recv.at[lr, j],
            device_id=(t, q), device_id_type=MESH)

    def own_copy(lr):
        return pltpu.make_async_copy(seeds.at[lr, c], xbuf.at[1, lr, b], own_sem.at[lr])

    def a_start(lr):
        for j in range(1, 8):
            a_copy(lr, j).start()
        own_copy(lr).start()

    goes = (has_high, has_low)
    comes = (has_low, has_high)

    def e_copy(side):
        return pltpu.make_async_remote_copy(
            src_ref=ebuf.at[1], dst_ref=ebuf.at[2 * side],
            send_sem=e_send.at[side], recv_sem=e_recv.at[side],
            device_id=(t + 1 - 2 * side, b), device_id_type=MESH)

    def x_copy(lr, j, side):
        q = lax.rem(b + 8 - j, 8)
        return pltpu.make_async_remote_copy(
            src_ref=xbuf.at[1, lr, q], dst_ref=xbuf.at[2 * side, lr, q],
            send_sem=x_send.at[lr, side, j], recv_sem=x_recv.at[lr, side, j],
            device_id=(t + 1 - 2 * side, b), device_id_type=MESH)

    def y_copy(lr, way, dt):
        q = mom_left if way else mom_right
        slot = 1 - dt
        return pltpu.make_async_remote_copy(
            src_ref=pack.at[lr, way], dst_ref=ybuf.at[slot, lr, way],
            send_sem=y_send.at[lr, way, slot], recv_sem=y_recv.at[lr, way, slot],
            device_id=(t + dt, q), device_id_type=MESH)

    a_start(0)
    loads[1].wait()
    unzip_seeds(1)
    a_start(1)

    loads[2].wait()
    values = []
    for n in range(3):
        col = pl.multiple_of(lax.rem(c + 7 + n, 8) * LANES, LANES)
        kinds = types[:, pl.ds(col, LANES)]
        value = jnp.zeros((32, LANES), F32)
        for kind in range(4):
            value = jnp.where(kinds == kind, levels[kind] * HOP, value)
        values.append(value)
    ebuf[1] = unzip(jnp.concatenate(values, axis=0)).reshape(3, 32, LANES)
    for side in range(2):
        @pl.when(goes[side])
        def _():
            e_copy(side).start()

    lane = lanes_of(8)

    def forward(lr):
        for j in range(8):
            if j == 0:
                q = b
                own_copy(lr).wait()
            else:
                q, arrival = a_arrival(lr, j)
                arrival.wait_recv()
            for side in range(2):
                @pl.when(goes[side])
                def _():
                    x_copy(lr, j, side).start()
            for way in range(2):
                packed = None
                for f in range(2):
                    for g in range(4):
                        slot = f * 4 + g
                        v = xbuf[1, lr, q, f, 8 * g:8 * g + 8, :]
                        source = 0 if way else HALF - EDGE
                        v = pltpu.roll(v, (EDGE * slot - source) % LANES, 1) if EDGE * slot != source else v
                        packed = v if packed is None else jnp.where(lane % HALF >= EDGE * slot, v, packed)
                pack[lr, way, q] = packed
        for way in range(2):
            y_copy(lr, way, 0).start()
            for side in range(2):
                @pl.when(goes[side])
                def _():
                    y_copy(lr, way, 1 - 2 * side).start()

    forward(0)
    forward(1)

    for side in range(2):
        @pl.when(comes[side])
        def _():
            e_copy(side).wait_recv()
    spread_energy(ebuf, energy)

    for lr in range(2):
        for way in range(2):
            y_copy(lr, way, 0).wait_recv()
        for side in range(2):
            @pl.when(comes[side])
            def _():
                for j in range(8):
                    x_copy(lr, j, side).wait_recv()
                for way in range(2):
                    y_copy(lr, way, 1 - 2 * side).wait_recv()
        fill(lr, t, xbuf, ybuf, state)
        run(lr, t, state, energy, arch)

    gram(arch, sums)

    def s_copy(j):
        s = lax.rem(t + j, 16)
        return pltpu.make_async_remote_copy(
            src_ref=sums.at[pl.ds(pl.multiple_of(16 * s, 16), 16), :], dst_ref=got.at[j],
            send_sem=s_send.at[j], recv_sem=s_recv.at[j], device_id=(s, b), device_id_type=MESH)

    for j in range(1, 16):
        s_copy(j).start()
    total = sums[pl.ds(pl.multiple_of(16 * t, 16), 16), :]
    for j in range(1, 16):
        s_copy(j).wait_recv()
        total = total + got[j]
    turned[:, 0:16] = jnp.transpose(total * scale)

    def m_copy(j):
        q = lax.rem(b + j, 8)
        return pltpu.make_async_remote_copy(
            src_ref=turned.at[pl.ds(pl.multiple_of(32 * q, 32), 32), :], dst_ref=parts.at[j],
            send_sem=m_send.at[j], recv_sem=m_recv.at[j], device_id=(t, q), device_id_type=MESH)

    for j in range(1, 8):
        m_copy(j).start()
    final = turned[pl.ds(pl.multiple_of(32 * b, 32), 32), :]
    for j in range(1, 8):
        m_copy(j).wait_recv()
        final = final + parts[j]
    out[...] = final[:, 0:16]

    for j in range(1, 16):
        s_copy(j).wait_send()
    for j in range(1, 8):
        m_copy(j).wait_send()
    for lr in range(2):
        for j in range(1, 8):
            a_copy(lr, j).wait_send()
        for way in range(2):
            y_copy(lr, way, 0).wait_send()
    for side in range(2):
        @pl.when(goes[side])
        def _():
            e_copy(side).wait_send()
            for lr in range(2):
                for j in range(8):
                    x_copy(lr, j, side).wait_send()
                for way in range(2):
                    y_copy(lr, way, 1 - 2 * side).wait_send()


def on_device(left_seeds, right_seeds, site_types, levels):
    dma = pltpu.SemaphoreType.DMA
    return pl.pallas_call(
        functools.partial(kernel, 1.0 / math.sqrt(512 * 1024)),
        out_shape=jax.ShapeDtypeStruct((32, 16), F32),
        in_specs=[pl.BlockSpec(memory_space=pl.ANY)] * 3 + [pl.BlockSpec(memory_space=pltpu.SMEM)],
        out_specs=pl.BlockSpec(memory_space=pltpu.VMEM),
        scratch_shapes=[
            pltpu.VMEM((2, 2, 32, 1024), F32),
            pltpu.VMEM((32, 1024), jnp.int32),
            pltpu.VMEM((2, 8, 2, 32, LANES), F32),
            pltpu.VMEM((3, 2, 8, 2, 32, LANES), F32),
            pltpu.VMEM((3, 2, 2, 8, 8, LANES), F32),
            pltpu.VMEM((3, 3, 32, LANES), F32),
            pltpu.VMEM((2, 2, 8, 8, LANES), F32),
            pltpu.VMEM((2, 96 + 2 * PAD, 2, 8, LANES), F32),
            pltpu.VMEM((96 + 2 * PAD, 2, 8, LANES), F32),
            pltpu.VMEM((2, 32, 256, LANES), F32),
            pltpu.VMEM((256, 256), F32),
            pltpu.VMEM((16, 16, 256), F32),
            pltpu.VMEM((256, LANES), F32),
            pltpu.VMEM((8, 32, LANES), F32),
            dma((3,)),
            dma((2, 8)), dma((2, 8)), dma((2,)),
            dma((2, 2, 8)), dma((2, 2, 8)),
            dma((2, 2, 3)), dma((2, 2, 3)),
            dma((2,)), dma((2,)),
            dma((16,)), dma((16,)), dma((8,)), dma((8,)),
        ],
        compiler_params=pltpu.CompilerParams(
            collective_id=0, has_side_effects=True, vmem_limit_bytes=48 << 20),
    )(left_seeds, right_seeds, site_types, levels)


def solution(mesh):
    return jax.shard_map(
        on_device,
        mesh=mesh,
        in_specs=(P("mom", None, "site", None), P("mom", None, "site", None), P("site", None), P()),
        out_specs=P("mom", "site"),
        check_vma=False,
    )
```

time: 1130 us -> 62.6 us (0.06)
  waiting for transfers between devices: 816 us -> 0 us
  starting transfers between devices: 139 us -> 0 us
  Pallas kernels: 0 us -> 58.3 us
  local copies, waits for them, and re-layouts: 59.1 us -> 4.13 us
  matrix products: 52 us -> 0 us
  other arithmetic: 38.1 us -> 0 us
  between operations: 13.5 us -> 0.01 us
    ppermute x69 -> x0, waiting for transfers between devices: 756 us -> none  [the longest x7 660 us: from_behind(): lax.ppermute(x, axis, [(i, (i + by) % devices) for i in range(devices)])]
    ppermute x69 -> x0, starting transfers between devices: 139 us -> none  [the longest x31 72.8 us: extended(): lax.ppermute(lax.slice_in_dim(block, 0, width, axis=dim), axis, backward)]
    reduce_scatter x1 -> x0, waiting for transfers between devices: 60.3 us -> none  [on_device(): lax.psum_scatter(partial_sums, 'site', scatter_dimension=1, tiled=True)]
    pallas_call x0 -> x1, Pallas kernels: none -> 58.3 us  [on_device(): pl.pallas_call(functools.partial(kernel, 1.0 / math.sqrt(512 * 1024)), ou...]
    dot_general x8 -> x0, matrix products: 52 us -> none  [product(): jnp.dot(left_block, right_piece.T, precision=lax.Precision.HIGHEST, prefe...]
    while x68 -> x0, local copies, waits for them, and re-layouts: 32.9 us -> none
    dynamic_update_slice x30 -> x0, other arithmetic: 26.2 us -> none  [on_device(): _, rest = lax.scan(step, (first, second), None, length=MB - 2)]
  transfers between devices with their start and end apart: 70 -> 0, of which waited for: 38 -> 0; matrix products, arithmetic and copies ran while one was open for 1% -> 0% of each run, Pallas kernels for 0% -> 0%
where the time goes in v1:
time: 62.6 us; the launch traced here: 62.5 us
  Pallas kernels  58.3 us (93%)
  local copies, waits for them, and re-layouts  4.13 us (7%)
    pallas_call x1, Pallas kernels, on_device(): pl.pallas_call(functools.partial(kernel, 1.0 / math.sqrt(512 * 1024)), ou...  58.3 us
    unnamed x8, local copies, waits for them, and re-layouts  3.46 us

profile of v1, /device:TPU:1, one launch (start us, length us, event | category | flops | bytes accessed | tf_op | source)
XLA Modules:
  0.0 62.5 jit_solution(2478038221308246079)
XLA Ops:
  0.0 0.0 copy-start
  0.0 0.9 %copy-done = f32[1,2,32,1024]{3,2,1,0:T(8,128)S(1)} copy-done((f32[1,2,32,1024]{3,2,1,0:T(8,128)S(1)}, f32[1,2,32,1024]{3,2,1,0:T(8,128)}, u32[]{:S(2)}) %copy-start) | copy-done | bytes 262168
  1.0 0.0 copy-start.1
  1.0 0.9 %copy-done.1 = f32[1,2,32,1024]{3,2,1,0:T(8,128)S(1)} copy-done((f32[1,2,32,1024]{3,2,1,0:T(8,128)S(1)}, f32[1,2,32,1024]{3,2,1,0:T(8,128)}, u32[]{:S(2)}) %copy-start.1) | copy-done | bytes 262168
  1.9 0.0 copy-start.2
  1.9 0.9 %copy-done.2 = s32[32,1024]{1,0:T(8,128)S(1)} copy-done((s32[32,1024]{1,0:T(8,128)S(1)}, s32[32,1024]{1,0:T(8,128)}, u32[]{:S(2)}) %copy-start.2) | copy-done | bytes 131096
  2.8 0.0 copy-start.3
  2.8 0.7 %copy-done.3 = f32[4]{0:T(128)S(1)} copy-done((f32[4]{0:T(128)S(1)}, f32[4]{0:T(128)}, u32[]{:S(2)}) %copy-start.3) | copy-done | bytes 40
  3.5 58.3 %shard_map.46 = f32[32,16]{1,0:T(8,128)S(1)} custom-call(f32[1,2,32,1024]{3,2,1,0:T(8,128)S(1)} %copy-done, f32[1,2,32,1024]{3,2,1,0:T(8,128)S(1)} %copy-done.1, s32[32,1024]{1,0:T(8,128)S(1)} %copy-done.2, f32[4]{0:T(128)S(1)} %copy-done.3), custom_call_target="tpu_custom_call" | custom-call | tf_op jit(solution)/shard_map/pallas_call | solution.py:368
  61.8 0.7 %copy.5 = f32[32,16]{0,1:T(8,128)} copy(f32[32,16]{1,0:T(8,128)S(1)} %shard_map.46) | data formatting | bytes 4096 | tf_op jit(solution)/shard_map/pallas_call | solution.py:368
Async XLA Ops:
  0.0 0.9 %copy-start = (f32[1,2,32,1024]{3,2,1,0:T(8,128)S(1)}, f32[1,2,32,1024]{3,2,1,0:T(8,128)}, u32[]{:S(2)}) copy-start(f32[1,2,32,1024]{3,2,1,0:T(8,128)} %left_ref.1) | copy-start | bytes 786436
  1.0 0.9 %copy-start.1 = (f32[1,2,32,1024]{3,2,1,0:T(8,128)S(1)}, f32[1,2,32,1024]{3,2,1,0:T(8,128)}, u32[]{:S(2)}) copy-start(f32[1,2,32,1024]{3,2,1,0:T(8,128)} %right_ref.1) | copy-start | bytes 786436
  1.9 0.9 %copy-start.2 = (s32[32,1024]{1,0:T(8,128)S(1)}, s32[32,1024]{1,0:T(8,128)}, u32[]{:S(2)}) copy-start(s32[32,1024]{1,0:T(8,128)} %types_ref.1) | copy-start | bytes 393220
  2.8 0.7 %copy-start.3 = (f32[4]{0:T(128)S(1)}, f32[4]{0:T(128)}, u32[]{:S(2)}) copy-start(f32[4]{0:T(128)} %levels.1) | copy-start | bytes 52

commit v2 on v1

--- a/solution.py
+++ b/solution.py
@@ -22,6 +22,10 @@
 
 def snake(b):
     return jnp.where(b < 4, b, 11 - b)
+
+
+def place(tile):
+    return tile ^ (((tile >> 2) & 1) << 1)
 
 
 def lanes_of(rows):
@@ -134,37 +138,50 @@
     save(lr, 31, 1, state, arch)
 
 
-def gram(arch, sums):
+def halves(arch, lr, i):
+    x = jnp.concatenate(
+        [jnp.concatenate([arch[lr, 2 * i + n, pl.ds(q, 32, stride=8), :] for q in range(8)], axis=0)
+         for n in range(2)], axis=1)
+    high = x.astype(BF16)
+    return high, (x - high.astype(F32)).astype(BF16)
+
+
+def split_left(arch, lefts):
+    def one(i, unused):
+        lefts[i, 0], lefts[i, 1] = halves(arch, 0, i)
+        return unused
+
+    lax.fori_loop(0, 16, one, 0, unroll=2)
+
+
+def gram(arch, lefts, sums):
     sums[...] = jnp.zeros_like(sums)
-
-    def halves(lr, r):
-        x = jnp.concatenate(
-            [jnp.concatenate([arch[lr, r + i, pl.ds(q, 32, stride=8), :] for q in range(8)], axis=0)
-             for i in range(2)], axis=1)
-        high = x.astype(BF16)
-        return high, (x - high.astype(F32)).astype(BF16)
 
     def product(a, c):
         return lax.dot_general(a, c, (((1,), (1,)), ((), ())), preferred_element_type=F32)
 
     def add(i, unused):
-        lh, ll = halves(0, 2 * i)
-        rh, rl = halves(1, 2 * i)
+        lh, ll = lefts[i, 0], lefts[i, 1]
+        rh, rl = halves(arch, 1, i)
         sums[...] += product(rh, lh) + product(rh, ll) + product(rl, lh)
         return unused
 
-    lax.fori_loop(0, 16, add, 0)
+    lax.fori_loop(0, 16, add, 0, unroll=4)
 
 
 def kernel(scale, left_ref, right_ref, types_ref, levels, out,
-           raw, types, seeds, xbuf, ybuf, ebuf, pack, state, energy, arch, sums, got, turned, parts,
+           raw, types, seeds, levels_here, xbuf, ybuf, ebuf, pack, state, energy, arch, lefts, sums, got, turned,
+           parts,
            in_sem, a_send, a_recv, own_sem, x_send, x_recv, y_send, y_recv, e_send, e_recv,
            s_send, s_recv, m_send, m_recv):
     t = lax.axis_index("site")
     b = lax.axis_index("mom")
     c = snake(b)
-    has_low = t > 0
-    has_high = t < 15
+    mine = place(t)
+    stays = mine == t
+    moves = mine != t
+    has_low = mine > 0
+    has_high = mine < 15
     mom_right = snake(lax.rem(c + 1, 8))
     mom_left = snake(lax.rem(c + 7, 8))
 
@@ -183,7 +200,12 @@
         @pl.when(there)
         def _():
             for q in (mom_left, mom_right):
-                pl.semaphore_signal(barrier, inc=1, device_id=(t + dt, q), device_id_type=MESH)
+                pl.semaphore_signal(barrier, inc=1, device_id=(place(mine + dt), q), device_id_type=MESH)
+
+    @pl.when(moves)
+    def _():
+        for j in range(1, 8):
+            pl.semaphore_signal(barrier, inc=1, device_id=(mine, lax.rem(b + j, 8)), device_id_type=MESH)
 
     def unzip_seeds(lr):
         x = jnp.concatenate(
@@ -192,21 +214,22 @@
 
     loads[0].wait()
     unzip_seeds(0)
-    pl.semaphore_wait(barrier, 22 + jnp.where(has_low, 2, 0) + jnp.where(has_high, 2, 0))
+    pl.semaphore_wait(
+        barrier, 22 + jnp.where(has_low, 2, 0) + jnp.where(has_high, 2, 0) + jnp.where(moves, 7, 0))
 
     def a_copy(lr, j):
         q = lax.rem(b + j, 8)
         return pltpu.make_async_remote_copy(
             src_ref=seeds.at[lr, snake(q)], dst_ref=xbuf.at[1, lr, b],
             send_sem=a_send.at[lr, j], recv_sem=a_recv.at[lr, j],
-            device_id=(t, q), device_id_type=MESH)
+            device_id=(mine, q), device_id_type=MESH)
 
     def a_arrival(lr, j):
         q = lax.rem(b + 8 - j, 8)
         return q, pltpu.make_async_remote_copy(
             src_ref=xbuf.at[1, lr, q], dst_ref=xbuf.at[1, lr, q],
             send_sem=a_send.at[lr, j], recv_sem=a_recv.at[lr, j],
-            device_id=(t, q), device_id_type=MESH)
+            device_id=(mine, q), device_id_type=MESH)
 
     def own_copy(lr):
         return pltpu.make_async_copy(seeds.at[lr, c], xbuf.at[1, lr, b], own_sem.at[lr])
@@ -214,23 +237,33 @@
     def a_start(lr):
         for j in range(1, 8):
             a_copy(lr, j).start()
-        own_copy(lr).start()
+
+        @pl.when(stays)
+        def _():
+            own_copy(lr).start()
+
+        @pl.when(moves)
+        def _():
+            a_copy(lr, 0).start()
 
     goes = (has_high, has_low)
     comes = (has_low, has_high)
 
-    def e_copy(side):
-        return pltpu.make_async_remote_copy(
-            src_ref=ebuf.at[1], dst_ref=ebuf.at[2 * side],
-            send_sem=e_send.at[side], recv_sem=e_recv.at[side],
-            device_id=(t + 1 - 2 * side, b), device_id_type=MESH)
+    def e_copy(dt):
+        return pltpu.make_async_remote_copy(
+            src_ref=levels_here, dst_ref=ebuf.at[1 - dt],
+            send_sem=e_send.at[1 - dt], recv_sem=e_recv.at[1 - dt],
+            device_id=(place(t + dt), b), device_id_type=MESH)
+
+    def e_keep():
+        return pltpu.make_async_copy(levels_here, ebuf.at[1], e_send.at[1])
 
     def x_copy(lr, j, side):
         q = lax.rem(b + 8 - j, 8)
         return pltpu.make_async_remote_copy(
             src_ref=xbuf.at[1, lr, q], dst_ref=xbuf.at[2 * side, lr, q],
             send_sem=x_send.at[lr, side, j], recv_sem=x_recv.at[lr, side, j],
-            device_id=(t + 1 - 2 * side, b), device_id_type=MESH)
+            device_id=(place(mine + 1 - 2 * side), b), device_id_type=MESH)
 
     def y_copy(lr, way, dt):
         q = mom_left if way else mom_right
@@ -238,7 +271,7 @@
         return pltpu.make_async_remote_copy(
             src_ref=pack.at[lr, way], dst_ref=ybuf.at[slot, lr, way],
             send_sem=y_send.at[lr, way, slot], recv_sem=y_recv.at[lr, way, slot],
-            device_id=(t + dt, q), device_id_type=MESH)
+            device_id=(place(mine + dt), q), device_id_type=MESH)
 
     a_start(0)
     loads[1].wait()
@@ -254,11 +287,23 @@
         for kind in range(4):
             value = jnp.where(kinds == kind, levels[kind] * HOP, value)
         values.append(value)
-    ebuf[1] = unzip(jnp.concatenate(values, axis=0)).reshape(3, 32, LANES)
-    for side in range(2):
-        @pl.when(goes[side])
-        def _():
-            e_copy(side).start()
+    levels_here[...] = unzip(jnp.concatenate(values, axis=0)).reshape(3, 32, LANES)
+
+    @pl.when(t < 15)
+    def _():
+        e_copy(1).start()
+
+    @pl.when(t > 0)
+    def _():
+        e_copy(-1).start()
+
+    @pl.when(moves)
+    def _():
+        e_copy(0).start()
+
+    @pl.when(stays)
+    def _():
+        e_keep().start()
 
     lane = lanes_of(8)
 
@@ -266,7 +311,14 @@
         for j in range(8):
             if j == 0:
                 q = b
-                own_copy(lr).wait()
+
+                @pl.when(stays)
+                def _():
+                    own_copy(lr).wait()
+
+                @pl.when(moves)
+                def _():
+                    a_copy(lr, 0).wait_recv()
             else:
                 q, arrival = a_arrival(lr, j)
                 arrival.wait_recv()
@@ -297,7 +349,16 @@
     for side in range(2):
         @pl.when(comes[side])
         def _():
-            e_copy(side).wait_recv()
+            e_copy(1 - 2 * side).wait_recv()
+
+    @pl.when(moves)
+    def _():
+        e_copy(0).wait_recv()
+
+    @pl.when(stays)
+    def _():
+        e_keep().wait()
+
     spread_energy(ebuf, energy)
 
     for lr in range(2):
@@ -310,10 +371,12 @@
                     x_copy(lr, j, side).wait_recv()
                 for way in range(2):
                     y_copy(lr, way, 1 - 2 * side).wait_recv()
-        fill(lr, t, xbuf, ybuf, state)
-        run(lr, t, state, energy, arch)
-
-    gram(arch, sums)
+        fill(lr, mine, xbuf, ybuf, state)
+        run(lr, mine, state, energy, arch)
+        if lr == 0:
+            split_left(arch, lefts)
+
+    gram(arch, lefts, sums)
 
     def s_copy(j):
         s = lax.rem(t + j, 16)
@@ -352,10 +415,24 @@
             a_copy(lr, j).wait_send()
         for way in range(2):
             y_copy(lr, way, 0).wait_send()
+
+    @pl.when(t < 15)
+    def _():
+        e_copy(1).wait_send()
+
+    @pl.when(t > 0)
+    def _():
+        e_copy(-1).wait_send()
+
+    @pl.when(moves)
+    def _():
+        e_copy(0).wait_send()
+        for lr in range(2):
+            a_copy(lr, 0).wait_send()
+
     for side in range(2):
         @pl.when(goes[side])
         def _():
-            e_copy(side).wait_send()
             for lr in range(2):
                 for j in range(8):
                     x_copy(lr, j, side).wait_send()
@@ -374,6 +451,7 @@
             pltpu.VMEM((2, 2, 32, 1024), F32),
             pltpu.VMEM((32, 1024), jnp.int32),
             pltpu.VMEM((2, 8, 2, 32, LANES), F32),
+            pltpu.VMEM((3, 32, LANES), F32),
             pltpu.VMEM((3, 2, 8, 2, 32, LANES), F32),
             pltpu.VMEM((3, 2, 2, 8, 8, LANES), F32),
             pltpu.VMEM((3, 3, 32, LANES), F32),
@@ -381,6 +459,7 @@
             pltpu.VMEM((2, 96 + 2 * PAD, 2, 8, LANES), F32),
             pltpu.VMEM((96 + 2 * PAD, 2, 8, LANES), F32),
             pltpu.VMEM((2, 32, 256, LANES), F32),
+            pltpu.VMEM((16, 2, 256, 256), BF16),
             pltpu.VMEM((256, 256), F32),
             pltpu.VMEM((16, 16, 256), F32),
             pltpu.VMEM((256, LANES), F32),
@@ -389,11 +468,11 @@
             dma((2, 8)), dma((2, 8)), dma((2,)),
             dma((2, 2, 8)), dma((2, 2, 8)),
             dma((2, 2, 3)), dma((2, 2, 3)),
-            dma((2,)), dma((2,)),
+            dma((3,)), dma((3,)),
             dma((16,)), dma((16,)), dma((8,)), dma((8,)),
         ],
         compiler_params=pltpu.CompilerParams(
-            collective_id=0, has_side_effects=True, vmem_limit_bytes=48 << 20),
+            collective_id=0, has_side_effects=True, vmem_limit_bytes=60 << 20),
     )(left_seeds, right_seeds, site_types, levels)
 
 

time: 62.6 us -> 54.1 us (0.86)
  Pallas kernels: 58.3 us -> 52.5 us
  local copies, waits for them, and re-layouts: 4.13 us -> 1.39 us
    pallas_call x1, Pallas kernels: 58.3 us -> 52.5 us  [on_device(): pl.pallas_call(functools.partial(kernel, 1.0 / math.sqrt(512 * 1024)), ou...]
    unnamed x8 -> x0, local copies, waits for them, and re-layouts: 3.46 us -> none
    pallas_call x1, local copies, waits for them, and re-layouts: 0.67 us -> 1.39 us  [on_device(): pl.pallas_call(functools.partial(kernel, 1.0 / math.sqrt(512 * 1024)), ou...]
where the time goes in v2:
time: 54.1 us; the launch traced here: 53.9 us
  Pallas kernels  52.5 us (97%)
  local copies, waits for them, and re-layouts  1.39 us (3%)
    pallas_call x1, Pallas kernels, on_device(): pl.pallas_call(functools.partial(kernel, 1.0 / math.sqrt(512 * 1024)), ou...  52.5 us
    pallas_call x1, local copies, waits for them, and re-layouts, on_device(): pl.pallas_call(functools.partial(kernel, 1.0 / math.sqrt(512 * 1024)), ou...  1.39 us

profile of v2, /device:TPU:1, one launch (start us, length us, event | category | flops | bytes accessed | tf_op | source)
XLA Modules:
  0.0 53.9 jit_solution(12144137787723477856)
XLA Ops:
  0.0 52.5 %shard_map.46 = f32[32,16]{1,0:T(8,128)} custom-call(f32[1,2,32,1024]{3,2,1,0:T(8,128)} %left_ref.1, f32[1,2,32,1024]{3,2,1,0:T(8,128)} %right_ref.1, s32[32,1024]{1,0:T(8,128)} %types_ref.1, f32[4]{0:T(128)} %levels.1), custom_call_target="tpu_custom_call" | custom-call | tf_op jit(solution)/shard_map/pallas_call | solution.py:445
  52.5 1.4 %copy.5 = f32[32,16]{0,1:T(8,128)} copy(f32[32,16]{1,0:T(8,128)} %shard_map.46) | data formatting | bytes 4096 | tf_op jit(solution)/shard_map/pallas_call | solution.py:445

commit v3 on v2

--- a/solution.py
+++ b/solution.py
@@ -10,6 +10,7 @@
 
 MB = 32
 HOP = 2.0 / 4.2
+HOP2 = HOP * HOP
 MESH = pl.DeviceIdType.MESH
 F32 = jnp.float32
 BF16 = jnp.bfloat16
@@ -17,7 +18,7 @@
 HALF = 64
 EDGE = 8
 PAD = 4
-PHASES = 5
+PHASES = (1,) * 15
 
 
 def snake(b):
@@ -51,12 +52,15 @@
 def spread_energy(ebuf, energy):
     lane = lanes_of(32)
     for tile in range(3):
-        own = ebuf[tile, 1]
-        halo = jnp.where(lane % HALF < 32, pltpu.roll(ebuf[tile, 2], HALF, 1), pltpu.roll(ebuf[tile, 0], HALF, 1))
-        for v in range(2):
-            value = jnp.where(lane < HALF, own, halo) if v == 0 else jnp.where(lane < HALF, halo, own)
+        own, right, left = ebuf[tile, 1], ebuf[tile, 2], ebuf[tile, 0]
+        turn = lambda x: pltpu.roll(x, HALF, 1)
+        even = jnp.where(lane < HALF, own, jnp.where(lane < 96, turn(right), turn(left)))
+        odd = jnp.where(lane < HALF, turn(own), jnp.where(lane < 96, right, left))
+        for v, value in enumerate((even, odd)):
             for r in range(32):
-                energy[PAD + 32 * tile + r, v] = jnp.broadcast_to(value[r:r + 1, :], (8, LANES))
+                row = jnp.broadcast_to(value[r:r + 1, :], (8, LANES))
+                energy[1, PAD + 32 * tile + r, v] = row
+                energy[0, PAD + 32 * tile + r, v] = row * HOP2
 
 
 def fill(lr, t, xbuf, ybuf, state):
@@ -74,13 +78,12 @@
                     slot = f * 4 + g
                     row = 32 * tile + 8 * g + r
                     own = xs[pl.ds(f * 32 + 8 * g + r, 8, stride=64), :]
-                    halo = jnp.where(
-                        lane % HALF < 32,
-                        pltpu.roll(high, HALF - EDGE * slot, 1),
-                        pltpu.roll(low, LANES - EDGE - EDGE * slot, 1))
-                    pair = (jnp.where(inner, own, halo), jnp.where(inner, halo, own))
+                    turn = lambda x, by: pltpu.roll(x, by % LANES, 1) if by % LANES else x
+                    even = jnp.where(lane < 96, turn(high, HALF - EDGE * slot), turn(low, LANES - EDGE - EDGE * slot))
+                    odd = jnp.where(lane < 96, turn(high, -EDGE * slot), turn(low, HALF - EDGE - EDGE * slot))
+                    pair = (jnp.where(inner, own, even), jnp.where(inner, turn(own, HALF), odd))
                     for v in range(2):
-                        new = pair[v]
+                        new = pair[v] * HOP if f else pair[v]
                         if row == 31:
                             new = jnp.where(t == 0, 0.0, new)
                         if row == 64:
@@ -94,11 +97,10 @@
     below, here = load(low - 1), load(low)
     for row in range(low, high):
         above = load(row + 1)
-        turn = (HALF, HALF) if row % 2 == 0 else (HALF + 1, HALF - 1)
         for v in range(2):
-            across = pltpu.roll(here[1 - v], turn[v], 1)
-            new = (energy[PAD + row, v] * here[v]
-                   + (above[v] + below[v] + across) * HOP - state[1 - p, PAD + row, v])
+            across = pltpu.roll(here[1 - v], LANES - 1 if v else 1, 1) if row % 2 else here[1 - v]
+            hops = above[v] + below[v] + across
+            new = energy[p, PAD + row, v] * here[v] + (hops if p else hops * HOP2) - state[1 - p, PAD + row, v]
             if row == 31:
                 new = jnp.where(t == 0, 0.0, new)
             if row == 64:
@@ -110,8 +112,8 @@
 
 
 def keep(lr, lane, row, k, below, here, above, arch):
-    join = lambda x: jnp.where(lane < HALF, x[0], x[1])
-    mine = join(above) - join(below) if lr else join(here)
+    even, odd = [jnp.where(lr == 1, above[v] - below[v], here[v]) for v in range(2)]
+    mine = jnp.where(lane < HALF, even, pltpu.roll(odd, HALF, 1))
     arch[lr, row - 32, pl.ds(pl.multiple_of(8 * k, 8), 8), :] = mine
 
 
@@ -124,17 +126,18 @@
 
 def run(lr, t, state, energy, arch):
     save(lr, 0, 0, state, arch)
-    pairs = 15 // PHASES
-    for phase in range(PHASES):
-        first = 2 * pairs * phase
+    k = 1
+    for pairs in PHASES:
+        first = k
 
         def double(i, unused):
-            k = first + 2 * i + 1
-            step(lr, t, k, 1, first + 1, 95 - first, state, energy, arch)
-            step(lr, t, k + 1, 0, first + 2, 94 - first, state, energy, arch)
+            now = first + 2 * i
+            step(lr, t, now, 1, first, 96 - first, state, energy, arch)
+            step(lr, t, now + 1, 0, first + 1, 95 - first, state, energy, arch)
             return unused
 
         lax.fori_loop(0, pairs, double, 0)
+        k += 2 * pairs
     save(lr, 31, 1, state, arch)
 
 
@@ -146,22 +149,14 @@
     return high, (x - high.astype(F32)).astype(BF16)
 
 
-def split_left(arch, lefts):
-    def one(i, unused):
-        lefts[i, 0], lefts[i, 1] = halves(arch, 0, i)
-        return unused
-
-    lax.fori_loop(0, 16, one, 0, unroll=2)
-
-
-def gram(arch, lefts, sums):
+def gram(arch, sums):
     sums[...] = jnp.zeros_like(sums)
 
     def product(a, c):
         return lax.dot_general(a, c, (((1,), (1,)), ((), ())), preferred_element_type=F32)
 
     def add(i, unused):
-        lh, ll = lefts[i, 0], lefts[i, 1]
+        lh, ll = halves(arch, 0, i)
         rh, rl = halves(arch, 1, i)
         sums[...] += product(rh, lh) + product(rh, ll) + product(rl, lh)
         return unused
@@ -169,8 +164,8 @@
     lax.fori_loop(0, 16, add, 0, unroll=4)
 
 
-def kernel(scale, left_ref, right_ref, types_ref, levels, out,
-           raw, types, seeds, levels_here, xbuf, ybuf, ebuf, pack, state, energy, arch, lefts, sums, got, turned,
+def kernel(scale, left_ref, right_ref, types_ref, levels_ref, out,
+           raw, levels, types, seeds, levels_here, xbuf, ybuf, ebuf, pack, state, energy, arch, sums, got, turned,
            parts,
            in_sem, a_send, a_recv, own_sem, x_send, x_recv, y_send, y_recv, e_send, e_recv,
            s_send, s_recv, m_send, m_recv):
@@ -187,7 +182,8 @@
 
     loads = [pltpu.make_async_copy(left_ref.at[0], raw.at[0], in_sem.at[0]),
              pltpu.make_async_copy(right_ref.at[0], raw.at[1], in_sem.at[1]),
-             pltpu.make_async_copy(types_ref, types, in_sem.at[2])]
+             pltpu.make_async_copy(types_ref, types, in_sem.at[2]),
+             pltpu.make_async_copy(levels_ref, levels, in_sem.at[3])]
     for load in loads:
         load.start()
 
@@ -279,13 +275,14 @@
     a_start(1)
 
     loads[2].wait()
+    loads[3].wait()
     values = []
     for n in range(3):
         col = pl.multiple_of(lax.rem(c + 7 + n, 8) * LANES, LANES)
         kinds = types[:, pl.ds(col, LANES)]
         value = jnp.zeros((32, LANES), F32)
         for kind in range(4):
-            value = jnp.where(kinds == kind, levels[kind] * HOP, value)
+            value = jnp.where(kinds == kind, levels[kind], value)
         values.append(value)
     levels_here[...] = unzip(jnp.concatenate(values, axis=0)).reshape(3, 32, LANES)
 
@@ -361,7 +358,7 @@
 
     spread_energy(ebuf, energy)
 
-    for lr in range(2):
+    def side_of(lr, unused):
         for way in range(2):
             y_copy(lr, way, 0).wait_recv()
         for side in range(2):
@@ -373,10 +370,10 @@
                     y_copy(lr, way, 1 - 2 * side).wait_recv()
         fill(lr, mine, xbuf, ybuf, state)
         run(lr, mine, state, energy, arch)
-        if lr == 0:
-            split_left(arch, lefts)
-
-    gram(arch, lefts, sums)
+        return unused
+
+    lax.fori_loop(0, 2, side_of, 0)
+    gram(arch, sums)
 
     def s_copy(j):
         s = lax.rem(t + j, 16)
@@ -390,21 +387,29 @@
     for j in range(1, 16):
         s_copy(j).wait_recv()
         total = total + got[j]
-    turned[:, 0:16] = jnp.transpose(total * scale)
+    for q in range(8):
+        column = LANES * (q // 4)
+        first, second = total[0:8, column:column + LANES], total[8:16, column:column + LANES]
+        shift = 32 * (q % 4)
+        turn = lambda x, by: pltpu.roll(x, by % LANES, 1) if by % LANES else x
+        turned[q] = jnp.where(lane < 32, turn(first, -shift), turn(second, 32 - shift))
 
     def m_copy(j):
         q = lax.rem(b + j, 8)
         return pltpu.make_async_remote_copy(
-            src_ref=turned.at[pl.ds(pl.multiple_of(32 * q, 32), 32), :], dst_ref=parts.at[j],
+            src_ref=turned.at[q], dst_ref=parts.at[j],
             send_sem=m_send.at[j], recv_sem=m_recv.at[j], device_id=(t, q), device_id_type=MESH)
 
     for j in range(1, 8):
         m_copy(j).start()
-    final = turned[pl.ds(pl.multiple_of(32 * b, 32), 32), :]
+    final = turned[b]
     for j in range(1, 8):
         m_copy(j).wait_recv()
         final = final + parts[j]
-    out[...] = final[:, 0:16]
+    block = jnp.transpose(final)
+    block = jnp.concatenate([block[0:32], block[32:64]], axis=1)
+    odds = (lax.broadcasted_iota(jnp.int32, (32, 16), 0) % 2) + (lax.broadcasted_iota(jnp.int32, (32, 16), 1) % 2)
+    out[...] = block * jnp.where(odds == 0, scale, jnp.where(odds == 1, scale / HOP, scale / HOP2))
 
     for j in range(1, 16):
         s_copy(j).wait_send()
@@ -445,10 +450,11 @@
     return pl.pallas_call(
         functools.partial(kernel, 1.0 / math.sqrt(512 * 1024)),
         out_shape=jax.ShapeDtypeStruct((32, 16), F32),
-        in_specs=[pl.BlockSpec(memory_space=pl.ANY)] * 3 + [pl.BlockSpec(memory_space=pltpu.SMEM)],
+        in_specs=[pl.BlockSpec(memory_space=pl.ANY)] * 4,
         out_specs=pl.BlockSpec(memory_space=pltpu.VMEM),
         scratch_shapes=[
             pltpu.VMEM((2, 2, 32, 1024), F32),
+            pltpu.SMEM((4,), F32),
             pltpu.VMEM((32, 1024), jnp.int32),
             pltpu.VMEM((2, 8, 2, 32, LANES), F32),
             pltpu.VMEM((3, 32, LANES), F32),
@@ -457,14 +463,13 @@
             pltpu.VMEM((3, 3, 32, LANES), F32),
             pltpu.VMEM((2, 2, 8, 8, LANES), F32),
             pltpu.VMEM((2, 96 + 2 * PAD, 2, 8, LANES), F32),
-            pltpu.VMEM((96 + 2 * PAD, 2, 8, LANES), F32),
+            pltpu.VMEM((2, 96 + 2 * PAD, 2, 8, LANES), F32),
             pltpu.VMEM((2, 32, 256, LANES), F32),
-            pltpu.VMEM((16, 2, 256, 256), BF16),
             pltpu.VMEM((256, 256), F32),
             pltpu.VMEM((16, 16, 256), F32),
-            pltpu.VMEM((256, LANES), F32),
-            pltpu.VMEM((8, 32, LANES), F32),
-            dma((3,)),
+            pltpu.VMEM((8, 8, LANES), F32),
+            pltpu.VMEM((8, 8, LANES), F32),
+            dma((4,)),
             dma((2, 8)), dma((2, 8)), dma((2,)),
             dma((2, 2, 8)), dma((2, 2, 8)),
             dma((2, 2, 3)), dma((2, 2, 3)),

time: 54.1 us -> 50.4 us (0.932)
  Pallas kernels: 52.5 us -> 48.8 us
    pallas_call x1, Pallas kernels: 52.5 us -> 48.8 us  [on_device(): pl.pallas_call(functools.partial(kernel, 1.0 / math.sqrt(512 * 1024)), ou...]
where the time goes in v3:
time: 50.4 us; the launch traced here: 50.2 us
  Pallas kernels  48.8 us (97%)
  local copies, waits for them, and re-layouts  1.39 us (3%)
    pallas_call x1, Pallas kernels, on_device(): pl.pallas_call(functools.partial(kernel, 1.0 / math.sqrt(512 * 1024)), ou...  48.8 us
    pallas_call x1, local copies, waits for them, and re-layouts, on_device(): pl.pallas_call(functools.partial(kernel, 1.0 / math.sqrt(512 * 1024)), ou...  1.39 us

profile of v3, /device:TPU:1, one launch (start us, length us, event | category | flops | bytes accessed | tf_op | source)
XLA Modules:
  0.0 50.2 jit_solution(18214722842166535089)
XLA Ops:
  0.0 48.8 %shard_map.46 = f32[32,16]{1,0:T(8,128)} custom-call(f32[1,2,32,1024]{3,2,1,0:T(8,128)} %left_ref.1, f32[1,2,32,1024]{3,2,1,0:T(8,128)} %right_ref.1, s32[32,1024]{1,0:T(8,128)} %types_ref.1, f32[4]{0:T(128)} %levels_ref.1), custom_call_target="tpu_custom_call" | custom-call | tf_op jit(solution)/shard_map/pallas_call | solution.py:450
  48.8 1.4 %copy.5 = f32[32,16]{0,1:T(8,128)} copy(f32[32,16]{1,0:T(8,128)} %shard_map.46) | data formatting | bytes 4096 | tf_op jit(solution)/shard_map/pallas_call | solution.py:450

commit v4 on v3

--- a/solution.py
+++ b/solution.py
@@ -477,7 +477,7 @@
             dma((16,)), dma((16,)), dma((8,)), dma((8,)),
         ],
         compiler_params=pltpu.CompilerParams(
-            collective_id=0, has_side_effects=True, vmem_limit_bytes=60 << 20),
+            collective_id=0, has_side_effects=True, vmem_limit_bytes=539 * (1 << 20) // 10),
     )(left_seeds, right_seeds, site_types, levels)
 
 

time: 50.4 us -> 49.6 us (0.984)
  Pallas kernels: 48.8 us -> 48.2 us
    pallas_call x1, local copies, waits for them, and re-layouts: 1.39 us -> 0.67 us  [on_device(): pl.pallas_call(functools.partial(kernel, 1.0 / math.sqrt(512 * 1024)), ou...]
    unnamed x0 -> x2, local copies, waits for them, and re-layouts: none -> 0.65 us
    pallas_call x1, Pallas kernels: 48.8 us -> 48.2 us  [on_device(): pl.pallas_call(functools.partial(kernel, 1.0 / math.sqrt(512 * 1024)), ou...]
where the time goes in v4:
time: 49.6 us; the launch traced here: 49.5 us
  Pallas kernels  48.2 us (97%)
  local copies, waits for them, and re-layouts  1.32 us (3%)
    pallas_call x1, Pallas kernels, on_device(): pl.pallas_call(functools.partial(kernel, 1.0 / math.sqrt(512 * 1024)), ou...  48.2 us

profile of v4, /device:TPU:1, one launch (start us, length us, event | category | flops | bytes accessed | tf_op | source)
XLA Modules:
  0.0 49.5 jit_solution(1214368568044463152)
XLA Ops:
  0.0 0.0 copy-start
  0.0 0.7 %copy-done = f32[4]{0:T(128)S(1)} copy-done((f32[4]{0:T(128)S(1)}, f32[4]{0:T(128)}, u32[]{:S(2)}) %copy-start) | copy-done | bytes 40
  0.7 48.2 %shard_map.46 = f32[32,16]{1,0:T(8,128)S(1)} custom-call(f32[1,2,32,1024]{3,2,1,0:T(8,128)} %left_ref.1, f32[1,2,32,1024]{3,2,1,0:T(8,128)} %right_ref.1, s32[32,1024]{1,0:T(8,128)} %types_ref.1, f32[4]{0:T(128)S(1)} %copy-done), custom_call_target="tpu_custom_call" | custom-call | tf_op jit(solution)/shard_map/pallas_call | solution.py:450
  48.8 0.7 %copy.5 = f32[32,16]{0,1:T(8,128)} copy(f32[32,16]{1,0:T(8,128)S(1)} %shard_map.46) | data formatting | bytes 4096 | tf_op jit(solution)/shard_map/pallas_call | solution.py:450
Async XLA Ops:
  0.0 0.7 %copy-start = (f32[4]{0:T(128)S(1)}, f32[4]{0:T(128)}, u32[]{:S(2)}) copy-start(f32[4]{0:T(128)} %levels_ref.1) | copy-start | bytes 52
